TPU v7x, 256 devices: a whole 4x4x8 slice. The times are simulated.
256 devices in a mesh: ctx: 64 (over x, z, core), ch: 4 (over y).
Axes of the slice: x: 4, y: 4, z: 8, core: 2. Of those that a mesh axis runs over, the one named last changes fastest.
Arguments:
- query_mr: bfloat16 [8192, 8192], P('ch', 'ctx'), may hold values from -18 to 18
- key_mr: bfloat16 [8192, 8192], P('ch', 'ctx'), may hold values from -6 to 6
- value_mr: bfloat16 [8192, 8192], P('ch', 'ctx'), may hold values from -6 to 6
- key_li: bfloat16 [8192, 8192], P('ch', 'ctx'), may hold values from -6 to 6
- cotangent: bfloat16 [8192, 8192], P('ch', 'ctx'), may hold values from -6 to 6
- norm_gain: float32 [8192], P('ch'), may hold values from 0.5 to 1.5
- filter_mr: float32 [8192, 128], P('ch'), may hold values from -0.5 to 0.5
- filter_li: float32 [8192, 8192], P('ch', 'ctx'), may hold values from -1 to 1
Outputs:
- grad_query: bfloat16 [8192, 8192], P('ch', 'ctx')
- grad_key: bfloat16 [8192, 8192], P('ch', 'ctx')
- grad_value: bfloat16 [8192, 8192], P('ch', 'ctx')
- grad_key_li: bfloat16 [8192, 8192], P('ch', 'ctx')
- grad_gain: float32 [8192], P('ch')
- grad_filter_mr: float32 [8192, 128], P('ch')
- grad_filter_li: float32 [8192, 8192], P('ch', 'ctx')
All inputs are finite; a program needn't handle non-finite values.
Results may differ from a plain program's by a relative error of at most 0.0085.
Values may be sent and summed in bfloat16 or wider, within the bound.
No kernel may reach another device: no remote copies, remote signals or barrier semaphores. Data moves between devices by JAX's collectives and lax.ppermute only.
A program may use at most 128 MiB of HBM per device.

v0:
```python
import math

import jax
import jax.numpy as jnp
from jax import lax
from jax.sharding import PartitionSpec as P

D = 8192


EPSILON = 1e-06
HIGHEST = lax.Precision.HIGHEST


def shifted(block, axis, distance):
    devices = range(lax.axis_size(axis))
    route = [(i - distance, i) for i in devices if i - distance in devices]
    return lax.ppermute(block, axis, route)


def causal_filter(padded, taps):
    count = taps.shape[1]
    out_len = padded.shape[1] - count + 1

    def causal_add_tap(index, total):
        piece = lax.dynamic_slice_in_dim(padded, count - 1 - index, out_len, 1)
        return total + lax.dynamic_slice_in_dim(taps, index, 1, 1) * piece

    return lax.fori_loop(
        0, count, causal_add_tap, jnp.zeros((padded.shape[0], out_len), padded.dtype)
    )


def later_filter(padded, taps):
    count = taps.shape[1]
    out_len = padded.shape[1] - count + 1

    def later_add_tap(index, total):
        piece = lax.dynamic_slice_in_dim(padded, index, out_len, 1)
        return total + lax.dynamic_slice_in_dim(taps, index, 1, 1) * piece

    return lax.fori_loop(
        0, count, later_add_tap, jnp.zeros((padded.shape[0], out_len), padded.dtype)
    )


def tap_gradient(padded, grads):
    out_len = grads.shape[1]
    count = padded.shape[1] - out_len + 1

    def one_tap(index):
        piece = lax.dynamic_slice_in_dim(padded, count - 1 - index, out_len, 1)
        return jnp.sum(grads * piece, axis=1)

    columns = lax.map(one_tap, jnp.arange(count, dtype=jnp.int32))
    return columns.T


def rounded(values):
    return lax.optimization_barrier(values.astype(jnp.bfloat16))


def dft_tables(radix):
    half_rows = jnp.arange(radix // 2, dtype=jnp.int32)
    columns = jnp.arange(radix, dtype=jnp.int32)
    outer_phase = (half_rows[:, None] * columns[None, :] % radix).astype(jnp.float32) * (
        2.0 * math.pi / radix
    )
    inner_index = jnp.arange(128, dtype=jnp.int32)
    inner_phase = (inner_index[:, None] * inner_index[None, :] % 128).astype(jnp.float32) * (
        2.0 * math.pi / 128
    )
    twist_phase = (columns[:, None] * inner_index[None, :] % (128 * radix)).astype(jnp.float32) * (
        2.0 * math.pi / (128 * radix)
    )
    return (
        jnp.cos(outer_phase),
        jnp.sin(outer_phase),
        jnp.cos(inner_phase),
        jnp.sin(inner_phase),
        jnp.cos(twist_phase),
        jnp.sin(twist_phase),
    )


def forward_spectrum(signal, tables):
    outer_cos, outer_sin, inner_cos, inner_sin, twist_cos, twist_sin = tables
    width = signal.shape[0]
    radix = outer_cos.shape[1]
    grid = signal.reshape(width, radix // 2, 128)
    first_re = jnp.einsum("cab,ak->ckb", grid, outer_cos, precision=HIGHEST)
    first_im = -jnp.einsum("cab,ak->ckb", grid, outer_sin, precision=HIGHEST)
    turn_re = first_re * twist_cos + first_im * twist_sin
    turn_im = first_im * twist_cos - first_re * twist_sin
    spec_re = jnp.einsum("ckb,bm->ckm", turn_re, inner_cos, precision=HIGHEST) + jnp.einsum(
        "ckb,bm->ckm", turn_im, inner_sin, precision=HIGHEST
    )
    spec_im = jnp.einsum("ckb,bm->ckm", turn_im, inner_cos, precision=HIGHEST) - jnp.einsum(
        "ckb,bm->ckm", turn_re, inner_sin, precision=HIGHEST
    )
    return (spec_re, spec_im)


def inverse_signal(spec_re, spec_im, tables):
    outer_cos, outer_sin, inner_cos, inner_sin, twist_cos, twist_sin = tables
    width = spec_re.shape[0]
    radix = outer_cos.shape[1]
    part_re = jnp.einsum("ckm,bm->ckb", spec_re, inner_cos, precision=HIGHEST) - jnp.einsum(
        "ckm,bm->ckb", spec_im, inner_sin, precision=HIGHEST
    )
    part_im = jnp.einsum("ckm,bm->ckb", spec_im, inner_cos, precision=HIGHEST) + jnp.einsum(
        "ckm,bm->ckb", spec_re, inner_sin, precision=HIGHEST
    )
    turn_re = part_re * twist_cos - part_im * twist_sin
    turn_im = part_im * twist_cos + part_re * twist_sin
    grid = jnp.einsum("ckb,ak->cab", turn_re, outer_cos, precision=HIGHEST) - jnp.einsum(
        "ckb,ak->cab", turn_im, outer_sin, precision=HIGHEST
    )
    return grid.reshape(width, -1) / (128.0 * radix)


def long_backward(signal, cotan, filt):
    radix = 2 * signal.shape[1] // 128
    tables = dft_tables(radix)
    signal_re, signal_im = forward_spectrum(signal.astype(jnp.float32), tables)
    cotan_re, cotan_im = forward_spectrum(cotan.astype(jnp.float32), tables)
    filter_re, filter_im = forward_spectrum(filt, tables)
    grad_signal = inverse_signal(
        cotan_re * filter_re + cotan_im * filter_im,
        cotan_im * filter_re - cotan_re * filter_im,
        tables,
    )
    grad_filter = inverse_signal(
        cotan_re * signal_re + cotan_im * signal_im,
        cotan_im * signal_re - cotan_re * signal_im,
        tables,
    )
    return (grad_signal.astype(jnp.bfloat16), grad_filter)


def local(query_mr, key_mr, value_mr, key_li, cotangent, norm_gain, filter_mr, filter_li):
    taps = filter_mr.shape[1]
    tok_count = query_mr.shape[1]
    long_filter = lax.all_to_all(filter_li, "ctx", split_axis=0, concat_axis=1, tiled=True)
    tails = jnp.stack([key_mr, value_mr])
    before = shifted(tails, "ctx", 1)
    prior = (before[0].astype(jnp.float32) * before[1].astype(jnp.float32))[:, 1:]
    query = query_mr.astype(jnp.float32)
    key_f = key_mr.astype(jnp.float32)
    value_f = value_mr.astype(jnp.float32)
    keyli_f = key_li.astype(jnp.float32)
    gain_col = norm_gain[:, None]
    padded = jnp.concatenate([prior, key_f * value_f], axis=1)
    conv_out = causal_filter(padded, filter_mr)
    mixed = rounded(query * conv_out).astype(jnp.float32)
    totals = lax.psum(jnp.sum(mixed * mixed, axis=0), "ch")
    inv_rms = lax.rsqrt(totals / D + EPSILON)
    normed = mixed * inv_rms
    scaled = normed * gain_col
    signal = (scaled * keyli_f).astype(jnp.bfloat16)
    moved_signal, moved_cotan = (
        lax.all_to_all(signal, "ctx", split_axis=0, concat_axis=1, tiled=True),
        lax.all_to_all(cotangent, "ctx", split_axis=0, concat_axis=1, tiled=True),
    )
    grad_moved, filter_grad_moved = long_backward(moved_signal, moved_cotan, long_filter)
    grad_signal = lax.all_to_all(grad_moved, "ctx", split_axis=1, concat_axis=0, tiled=True).astype(
        jnp.float32
    )
    grad_scaled = grad_signal * keyli_f
    grad_key_li = (grad_signal * scaled).astype(jnp.bfloat16)
    gain_terms = jnp.sum(grad_scaled * normed, axis=1)
    grad_normed = grad_scaled * gain_col
    project = lax.psum(jnp.sum(grad_normed * normed, axis=0), "ch")
    grad_mixed = inv_rms * (grad_normed - normed * (project / D))
    grad_query = (grad_mixed * conv_out).astype(jnp.bfloat16)
    grad_conv = grad_mixed * query
    after = shifted(grad_conv.astype(jnp.bfloat16), "ctx", -1).astype(grad_conv.dtype)
    later = jnp.concatenate([grad_conv, after[:, : taps - 1]], axis=1)
    grad_product = later_filter(later, filter_mr)
    grad_key = (grad_product * value_f).astype(jnp.bfloat16)
    grad_value = (grad_product * key_f).astype(jnp.bfloat16)
    filter_terms = tap_gradient(padded, grad_conv)
    grad_filter_mr, grad_gain = lax.psum((filter_terms, gain_terms), "ctx")
    grad_filter_li = lax.all_to_all(
        filter_grad_moved.astype(jnp.bfloat16), "ctx", split_axis=1, concat_axis=0, tiled=True
    ).astype(filter_grad_moved.dtype)
    return (
        grad_query,
        grad_key,
        grad_value,
        grad_key_li,
        grad_gain,
        grad_filter_mr,
        grad_filter_li,
    )


def solution(mesh):
    in_specs = (
        P("ch", "ctx"),
        P("ch", "ctx"),
        P("ch", "ctx"),
        P("ch", "ctx"),
        P("ch", "ctx"),
        P("ch"),
        P("ch", None),
        P("ch", "ctx"),
    )
    out_specs = (
        P("ch", "ctx"),
        P("ch", "ctx"),
        P("ch", "ctx"),
        P("ch", "ctx"),
        P("ch"),
        P("ch", None),
        P("ch", "ctx"),
    )
    return jax.shard_map(local, mesh=mesh, in_specs=in_specs, out_specs=out_specs, check_vma=False)
```

profile of v0, /device:TPU:8, one launch (start us, length us, event | category | flops | bytes accessed | tf_op | source)
XLA Modules:
  0.0 1517.6 jit_solution(17653799522692053863)
XLA Ops:
  7.2 11.9 all-to-all-start
  21.6 3.0 collective-permute-start
  24.6 2.5 copy.24
  28.5 9.2 all-to-all-done
  37.7 6.0 all-to-all-start.1
  48.3 3.5 fusion.18
  51.8 3.5 fusion.43
  57.7 228.2 %while.43 = (s32[]{:T(128)}, f32[2048,128]{1,0:T(8,128)S(1)}, f32[2048,128]{0,1:T(8,128)}, f32[2048,255]{1,0:T(8,128)S(1)}, s32[]{:T(128)}, /*index=5*/s32[]{:T(128)}, s32[]{:T(128)}, s32[]{:T(128)}) while((s32[]{:T(128)}, f32[2048,128]{1,0:T(8,128)S(1)}, f32[2048,128]{0,1:T(8,128)}, f32[2048,255]{1,0:T(8,128)S(1)}, s32[]{:T(128)}, ...), condition=%wide.region_1.0_spmd.clone, body=%wide.region_0.0_spmd.clone.sunk | while | flops 786439 | bytes 3170453 | solution.py:29
  288.6 8.7 psum.28
  299.6 10.6 all-to-all-start.3
  310.2 3.6 fusion.97
  313.9 3.6 fusion.99
  322.0 3.5 fusion.46
  325.5 3.8 fusion.49
  338.4 2.7 fusion.55
  341.9 3.2 multiply_subtract_fusion
  347.2 3.4 fusion.140
  350.6 3.4 convolution_add_fusion
  367.3 10.8 all-to-all-start.2
  378.1 4.5 convolution_subtract_fusion
  387.1 8.1 all-to-all-done.2
  395.2 6.6 all-to-all-start.4
  404.2 10.2 psum.29
  414.4 3.3 fusion.331
  419.0 515.1 %while.42 = (s32[]{:T(128)}, f32[128,2048]{1,0:T(8,128)}, s32[128]{0:T(128)S(1)}, f32[2048,255]{1,0:T(8,128)S(1)}, f32[2048,128]{1,0:T(8,128)S(1)}, /*index=5*/s32[]{:T(128)}, s32[1]{0:T(128)}, s32[]{:T(128)}, s32[1]{0:T(128)}) while((s32[]{:T(128)}, f32[128,2048]{1,0:T(8,128)}, s32[128]{0:T(128)S(1)}, f32[2048,255]{1,0:T(8,128)S(1)}, ...), condition=%wide.region_12.13_spmd, body=%wide.region_10.12_spmd.sunk | while | flops 522246 | bytes 2121887 | solution.py:55
  934.0 2.5 copy.29
  938.8 133.5 %psum.30 = f32[2048]{0:T(1024)} all-reduce(f32[2048]{0:T(1024)S(1)} %get-tuple-element.310), channel_id=1, replica_groups=mesh['ctx'=64,'ch'=4] {'ctx'}, use_global_device_ids=true, to_apply=%region_9.10 | all-reduce | flops 2048 | bytes 16384 | tf_op jit(solution)/shard_map/psum | solution.py:183
  1075.0 432.0 %while.44 = (s32[]{:T(128)}, f32[2048,128]{1,0:T(8,128)S(1)}, f32[2048,128]{0,1:T(8,128)}, f32[2048,255]{1,0:T(8,128)}, s32[]{:T(128)}, /*index=5*/s32[]{:T(128)}) while((s32[]{:T(128)}, f32[2048,128]{1,0:T(8,128)S(1)}, f32[2048,128]{0,1:T(8,128)}, f32[2048,255]{1,0:T(8,128)}, s32[]{:T(128)}, /*index=5*/s32[]{:T(128)}) %tuple.120), condition=%wide.region_7.8_spmd.clone, body=%wide.region_6.7_spmd.clone.sunk | while | flops 786435 | bytes 3170391 | solution.py:42
  1075.9 2.5 select_add_fusion.5
  1086.1 2.5 select_add_fusion.5
  1096.3 2.5 select_add_fusion.5
  1103.0 2.5 select_add_fusion.5
  (985 shorter events, 1053.4 us)
Async XLA Ops:
  7.2 30.5 %all-to-all-start = ((bf16[64,32,128]{2,1,0:T(8,128)(2,1)}), bf16[64,32,128]{2,1,0:T(8,128)(2,1)S(1)}, u32[]{:S(2)}, u32[]{:S(2)}) async-start(bf16[64,32,128]{2,1,0:T(8,128)(2,1)} %bitcast.190), calls=%async_computation | async-start | bytes 1048576 | tf_op jit(solution)/shard_map/all_to_all | solution.py:163
  19.1 8.2 copy-start.15
  19.1 8.2 copy-start.17
  21.6 33.7 %collective-permute-start = (bf16[2,2048,128]{2,1,0:T(8,128)(2,1)}, bf16[2,2048,128]{2,1,0:T(8,128)(2,1)}, u32[]{:S(2)}, u32[]{:S(2)}) collective-permute-start(bf16[2,2048,128]{2,1,0:T(8,128)(2,1)} %pad_maximum_fusion.2), channel_id=1, source_target_pairs={{0,4},{4,8},{8,12},{12,16},{16,20},{20,24},{24,28},{28,32},{32,36}... | collective-permute-start | bytes 3145736 | tf_op jit(solution)/shard_map/ppermute | solution.py:18
  37.7 261.9 %all-to-all-start.1 = ((f32[64,32,128]{2,1,0:T(8,128)}), f32[64,32,128]{2,1,0:T(8,128)}, u32[]{:S(2)}, u32[]{:S(2)}) async-start(f32[64,32,128]{2,1,0:T(8,128)} %bitcast.186), calls=%async_computation.1 | async-start | bytes 2097152 | tf_op jit(solution)/shard_map/all_to_all | solution.py:144
  44.9 6.9 copy-start
  46.1 5.7 copy-start.2
  55.3 1.7 copy-start.19
  285.9 13.7 copy-start.4
  285.9 11.3 copy-start.20
  287.5 0.8 copy-start.8
  299.6 29.7 %all-to-all-start.3 = ((bf16[64,32,128]{2,1,0:T(8,128)(2,1)}), bf16[64,32,128]{2,1,0:T(8,128)(2,1)S(1)}, u32[]{:S(2)}, u32[]{:S(2)}) async-start(bf16[64,32,128]{2,1,0:T(8,128)(2,1)} %bitcast.184), calls=%async_computation.3 | async-start | bytes 1048576 | tf_op jit(solution)/shard_map/all_to_all | solution.py:162
  336.1 5.1 copy-start.12
  336.1 5.1 copy-start.13
  338.4 2.8 copy-start.1
  338.4 2.8 copy-start.3
  338.4 2.8 copy-start.10
  338.4 3.4 copy-start.11
  345.1 2.1 copy-start.6
  367.3 27.9 %all-to-all-start.2 = ((bf16[32,64,128]{2,0,1:T(8,128)(2,1)}), bf16[32,64,128]{2,0,1:T(8,128)(2,1)}, u32[]{:S(2)}, u32[]{:S(2)}) async-start(bf16[32,64,128]{2,0,1:T(8,128)(2,1)} %copy.27), calls=%async_computation.2 | async-start | bytes 1048576 | tf_op jit(solution)/shard_map/all_to_all | solution.py:166
  378.1 4.5 copy-start.7
  385.9 15.9 %copy-start.9 = (bf16[2048,128]{1,0:T(8,128)(2,1)S(1)}, bf16[2048,128]{1,0:T(8,128)(2,1)}, u32[]{:S(2)}) copy-start(bf16[2048,128]{1,0:T(8,128)(2,1)} %copy-done.8) | copy-start | bytes 1572868
  385.9 15.9 %copy-start.14 = (bf16[2048,128]{1,0:T(8,128)(2,1)S(1)}, bf16[2048,128]{1,0:T(8,128)(2,1)}, u32[]{:S(2)}) copy-start(bf16[2048,128]{1,0:T(8,128)(2,1)} %param.17) | copy-start | bytes 1572868
  395.2 541.4 %all-to-all-start.4 = ((bf16[32,64,128]{2,0,1:T(8,128)(2,1)}), bf16[32,64,128]{2,0,1:T(8,128)(2,1)}, u32[]{:S(2)}, u32[]{:S(2)}) async-start(bf16[32,64,128]{2,0,1:T(8,128)(2,1)} %copy.31), calls=%async_computation.4 | async-start | bytes 1048576 | tf_op jit(solution)/shard_map/all_to_all | solution.py:184
  401.8 1106.5 %all-reduce.2.cloned.1.call-start = ((), (), s32[]{:S(2)}) async-start(), calls=%async_computation.5 | async-start | bytes 2097152 | tf_op jit(solution)/shard_map/psum | solution.py:183
  417.7 654.6 %collective-permute-start.1 = (bf16[2048,128]{1,0:T(8,128)(2,1)}, bf16[2048,128]{1,0:T(8,128)(2,1)}, u32[]{:S(2)}, u32[]{:S(2)}) collective-permute-start(bf16[2048,128]{1,0:T(8,128)(2,1)} %get-tuple-element.338), channel_id=1, source_target_pairs={{4,0},{8,4},{12,8},{16,12},{20,16},{24,20},{28,24},{32,28},{36,32}... | collective-permute-start | bytes 1572872 | tf_op jit(solution)/shard_map/ppermute | solution.py:18
  1073.4 1.6 copy-start.5
  1075.0 432.0 %copy-start.16 = (bf16[2048,128]{1,0:T(8,128)(2,1)S(1)}, bf16[2048,128]{1,0:T(8,128)(2,1)}, u32[]{:S(2)}) copy-start(bf16[2048,128]{1,0:T(8,128)(2,1)} %param.16) | copy-start | bytes 1572868
  1075.0 432.0 %copy-start.18 = (bf16[2048,128]{1,0:T(8,128)(2,1)S(1)}, bf16[2048,128]{1,0:T(8,128)(2,1)}, u32[]{:S(2)}) copy-start(bf16[2048,128]{1,0:T(8,128)(2,1)} %param.15) | copy-start | bytes 1572868
Sparse Core Ops, SparseCore 0:
  936.7 185.6 all-reduce.1
where the time goes:
time: 1550 us; the launch traced here: 1520 us
  other arithmetic  539 us (35%)
  local copies, waits for them, and re-layouts  496 us (32%)
  loops' own time  173 us (11%)
  blocking collectives  152 us (10%)
  matrix products  74.4 us (5%)
  starting transfers between devices  50.2 us (3%)
  waiting for transfers between devices  17.4 us (1%)
    add x128, other arithmetic, later_add_tap(): return total + lax.dynamic_slice_in_dim(taps, index, 1, 1) * piece  320 us
    dynamic_update_slice x128, local copies, waits for them, and re-layouts, tap_gradient(): columns = lax.map(one_tap, jnp.arange(count, dtype=jnp.int32))  192 us
    another operation x1, loops' own time, tap_gradient(): columns = lax.map(one_tap, jnp.arange(count, dtype=jnp.int32))  167 us
    psum x1, blocking collectives, local(): grad_filter_mr, grad_gain = lax.psum((filter_terms, gain_terms), 'ctx')  134 us
    add x128, other arithmetic, causal_add_tap(): return total + lax.dynamic_slice_in_dim(taps, index, 1, 1) * piece  116 us
    dynamic_slice x128, local copies, waits for them, and re-layouts, later_add_tap(): return total + lax.dynamic_slice_in_dim(taps, index, 1, 1) * piece  109 us
    dynamic_slice x128, local copies, waits for them, and re-layouts, causal_add_tap(): return total + lax.dynamic_slice_in_dim(taps, index, 1, 1) * piece  109 us
    reduce_sum x128, other arithmetic, one_tap(): return jnp.sum(grads * piece, axis=1)  81.7 us
  transfers between devices with their start and end apart: 8, of which 2 were waited for; matrix products, arithmetic and copies ran while one was open for 70% of the time, Pallas kernels for 0%

commit v1 on v0

v1 whole, which is shorter than its diff:
```python
import functools
import math

import jax
import jax.numpy as jnp
import numpy as np
from jax import lax
from jax.experimental import pallas as pl
from jax.experimental.pallas import tpu as pltpu
from jax.sharding import PartitionSpec as P

D = 8192
LANES = 128
EPSILON = 1e-06
BF16 = jnp.bfloat16
F32 = jnp.float32


def halves(table):
    high = table.astype(np.float32).astype(BF16)
    low = (table - high.astype(np.float64)).astype(np.float32).astype(BF16)
    return jnp.asarray(high), jnp.asarray(low)


def short_tables():
    place = np.arange(2 * LANES)
    angle = 2.0 * math.pi / (2 * LANES) * place[:, None] * (np.arange(LANES)[None, :] + 0.5)
    ahead = np.concatenate([np.cos(angle), -np.sin(angle)], axis=1)
    return halves(ahead) + halves(ahead.T / LANES)


def long_tables(blocks):
    radix = 2 * blocks
    total = radix * LANES
    half = np.arange(blocks) + 0.5
    outer = 2.0 * math.pi / radix * half[:, None] * np.arange(blocks)[None, :]
    first = np.concatenate([np.cos(outer), -np.sin(outer)], axis=0)
    twist = 2.0 * math.pi / total * half[:, None] * np.arange(LANES)[None, :]
    inner = 2.0 * math.pi / LANES * (np.arange(LANES)[:, None] * np.arange(LANES)[None, :] % LANES)
    cosine, sine = np.cos(inner), np.sin(inner)
    second = np.block([[cosine, -sine], [sine, cosine]])
    first_high, first_low = halves(first)
    last_high, last_low = halves(first.T * (2.0 / total))
    return (
        jnp.concatenate([first_high, first_low], axis=1),
        jnp.asarray(np.cos(twist), F32),
        jnp.asarray(np.sin(twist), F32),
        *halves(second),
        *halves(second.T),
        jnp.concatenate([last_high, last_high, last_low], axis=1),
    )


def dot(left, right):
    return jnp.dot(left, right, preferred_element_type=F32)


def split(values):
    high = values.astype(BF16)
    return high, (values - high.astype(F32)).astype(BF16)


def dot3(values, high, low):
    values_high, values_low = split(values)
    return dot(values_high, high) + dot(values_low, high) + dot(values_high, low)


def mr_forward_kernel(
    key, value, prior, query, key_li, gain, taps, ahead_high, ahead_low, back_high, back_low,
    conv_out, mixed_out, scaled_out, gated_out, window_spec, taps_spec, squares,
):
    product = key[...].astype(F32) * value[...].astype(F32)
    window = jnp.concatenate([prior[...].astype(F32), product], axis=1)
    spec = dot3(window, ahead_high[...], ahead_low[...])
    filt = dot3(taps[...], ahead_high[:LANES], ahead_low[:LANES])
    spec_re, spec_im = spec[:, :LANES], spec[:, LANES:]
    filt_re, filt_im = filt[:, :LANES], filt[:, LANES:]
    passed = jnp.concatenate(
        [spec_re * filt_re - spec_im * filt_im, spec_re * filt_im + spec_im * filt_re], axis=1
    )
    conv = dot3(passed, back_high[:, LANES:], back_low[:, LANES:])
    mixed_bf = (query[...].astype(F32) * conv).astype(BF16)
    mixed = mixed_bf.astype(F32)
    gain_col = gain[...]
    conv_out[...] = conv
    mixed_out[...] = mixed_bf
    scaled_out[...] = mixed * gain_col
    gated_out[...] = key_li[...].astype(F32) * gain_col
    window_spec[...] = spec
    taps_spec[...] = filt

    @pl.when(pl.program_id(0) == 0)
    def _():
        squares[...] = jnp.zeros_like(squares)

    squares[...] += jnp.sum(mixed * mixed, axis=0, keepdims=True)


def mr_backward_kernel(
    grad_signal, gated, mixed, conv, query, inv_rms, project, window_spec, taps_spec,
    ahead_high, ahead_low, back_high, back_low,
    grad_query, taps_grad, before_grad, own_grad,
):
    inv = inv_rms[...]
    normed = mixed[...].astype(F32) * inv
    grad_mixed = inv * (grad_signal[...].astype(F32) * gated[...] - normed * project[...])
    grad_query[...] = (grad_mixed * conv[...]).astype(BF16)
    grad_conv = grad_mixed * query[...].astype(F32)
    spec = dot3(grad_conv, ahead_high[LANES:], ahead_low[LANES:])
    spec_re, spec_im = spec[:, :LANES], spec[:, LANES:]

    def against(other):
        other_re, other_im = other[:, :LANES], other[:, LANES:]
        return jnp.concatenate(
            [spec_re * other_re + spec_im * other_im, spec_im * other_re - spec_re * other_im],
            axis=1,
        )

    taps_grad[...] = dot3(
        against(window_spec[...]), back_high[:, :LANES], back_low[:, :LANES]
    ).astype(BF16)
    both = dot3(against(taps_spec[...]), back_high[...], back_low[...])
    before_grad[...] = both[:, :LANES].astype(BF16)
    own_grad[...] = both[:, LANES:]


ROWS = 256


def row_spec(width=LANES):
    return pl.BlockSpec((ROWS, width), lambda i: (i, 0))


def whole_spec(shape):
    return pl.BlockSpec(shape, lambda i: (0,) * len(shape))


def mr_forward(key, value, prior, query, key_li, gain, taps, tables):
    rows = key.shape[0]
    wide = jax.ShapeDtypeStruct((rows, 2 * LANES), F32)
    full = jax.ShapeDtypeStruct((rows, LANES), F32)
    half = jax.ShapeDtypeStruct((rows, LANES), BF16)
    return pl.pallas_call(
        mr_forward_kernel,
        grid=(rows // ROWS,),
        in_specs=[row_spec()] * 5
        + [row_spec(1), row_spec()]
        + [whole_spec(table.shape) for table in tables],
        out_specs=[row_spec()] * 4 + [row_spec(2 * LANES)] * 2 + [whole_spec((1, LANES))],
        out_shape=[full, half, full, full, wide, wide, jax.ShapeDtypeStruct((1, LANES), F32)],
        name="mr_forward",
    )(key, value, prior, query, key_li, gain, taps, *tables)


def mr_backward(
    grad_signal, gated, mixed, conv, query, inv_rms, project, window_spec, taps_spec, tables
):
    rows = mixed.shape[0]
    half = jax.ShapeDtypeStruct((rows, LANES), BF16)
    return pl.pallas_call(
        mr_backward_kernel,
        grid=(rows // ROWS,),
        in_specs=[row_spec()] * 5
        + [whole_spec((1, LANES))] * 2
        + [row_spec(2 * LANES)] * 2
        + [whole_spec(table.shape) for table in tables],
        out_specs=[row_spec()] * 4,
        out_shape=[half, half, half, jax.ShapeDtypeStruct((rows, LANES), F32)],
        name="mr_backward",
    )(grad_signal, gated, mixed, conv, query, inv_rms, project, window_spec, taps_spec, *tables)


GROUP = 4


def channel_rows(channel, blocks, width):
    return pl.ds(channel, blocks, stride=width)


def to_spectrum(flat, channels, blocks, width, first, cosine, sine, high, low):
    pieces = [flat[channel_rows(c, blocks, width), :].astype(BF16) for c in channels]
    grid = jnp.concatenate(pieces, axis=1)
    outer = dot(first[...], jnp.concatenate([grid, grid], axis=0))
    cos, sin = cosine[...], sine[...]
    turned = []
    for at in range(len(channels)):
        lanes = slice(at * LANES, (at + 1) * LANES)
        real, imag = outer[:blocks, lanes], outer[blocks:, lanes]
        turned.append(
            jnp.concatenate([real * cos + imag * sin, imag * cos - real * sin], axis=1)
        )
    return dot3(jnp.concatenate(turned, axis=0), high[...], low[...])


def from_spectrum(spec, count, blocks, high, low, cosine, sine, last):
    inner = dot3(spec, high[...], low[...])
    cos, sin = cosine[...], sine[...]
    turned = []
    for at in range(count):
        rows = slice(at * blocks, (at + 1) * blocks)
        real, imag = inner[rows, :LANES], inner[rows, LANES:]
        turned.append(
            jnp.concatenate([real * cos - imag * sin, imag * cos + real * sin], axis=0)
        )
    top, rest = split(jnp.concatenate(turned, axis=1))
    return dot(last[...], jnp.concatenate([top, rest, top], axis=0))


def times_conj(left, right):
    left_re, left_im = left[:, :LANES], left[:, LANES:]
    right_re, right_im = right[:, :LANES], right[:, LANES:]
    return jnp.concatenate(
        [left_re * right_re + left_im * right_im, left_im * right_re - left_re * right_im], axis=1
    )


def signal_grad_kernel(
    blocks, width, cotan, filt, first, cosine, sine, high, low, back_high, back_low, last,
    grad_out, cotan_spec, cotan_flat, filt_flat, grad_flat,
):
    cotan_flat[...] = cotan[...].astype(F32)
    filt_flat[...] = filt[...].astype(F32)

    def one_group(step, carry):
        channels = [step * GROUP + at for at in range(GROUP)]
        spectrum = functools.partial(
            to_spectrum, channels=channels, blocks=blocks, width=width,
            first=first, cosine=cosine, sine=sine, high=high, low=low,
        )
        moved = spectrum(cotan_flat)
        rows = pl.ds(pl.multiple_of(step * (GROUP * blocks), GROUP * blocks), GROUP * blocks)
        cotan_spec[rows, :] = moved
        grads = from_spectrum(
            times_conj(moved, spectrum(filt_flat)),
            GROUP, blocks, back_high, back_low, cosine, sine, last,
        )
        for at, channel in enumerate(channels):
            lanes = slice(at * LANES, (at + 1) * LANES)
            grad_flat[channel_rows(channel, blocks, width), :] = grads[:, lanes]
        return carry

    lax.fori_loop(0, width // GROUP, one_group, 0)
    grad_out[...] = grad_flat[...].astype(BF16)


def filter_grad_kernel(
    blocks, width, signal, cotan_spec, grad_signal, first, cosine, sine, high, low, back_high,
    back_low, last, grad_out, gain_terms, signal_flat, grad_flat,
):
    signal_flat[...] = signal[...].astype(F32)
    terms = signal_flat[...] * grad_signal[...].astype(F32)
    gain_terms[...] = jnp.sum(terms.reshape(blocks, width, LANES), axis=0)

    def one_group(step, carry):
        channels = [step * GROUP + at for at in range(GROUP)]
        moved = to_spectrum(
            signal_flat, channels, blocks, width, first, cosine, sine, high, low
        )
        rows = pl.ds(pl.multiple_of(step * (GROUP * blocks), GROUP * blocks), GROUP * blocks)
        grads = from_spectrum(
            times_conj(cotan_spec[rows, :], moved),
            GROUP, blocks, back_high, back_low, cosine, sine, last,
        )
        for at, channel in enumerate(channels):
            lanes = slice(at * LANES, (at + 1) * LANES)
            grad_flat[channel_rows(channel, blocks, width), :] = grads[:, lanes]
        return carry

    lax.fori_loop(0, width // GROUP, one_group, 0)
    grad_out[...] = grad_flat[...].astype(BF16)


VMEM = pl.BlockSpec(memory_space=pltpu.VMEM)
LIMIT = pltpu.CompilerParams(vmem_limit_bytes=48 * 1024 * 1024)


def signal_grad(cotan, filt, blocks, tables):
    rows = cotan.shape[0]
    flat = pltpu.VMEM((rows, LANES), F32)
    return pl.pallas_call(
        functools.partial(signal_grad_kernel, blocks, rows // blocks),
        in_specs=[VMEM] * (2 + len(tables)),
        out_specs=[VMEM] * 2,
        out_shape=[
            jax.ShapeDtypeStruct((rows, LANES), BF16),
            jax.ShapeDtypeStruct((rows, 2 * LANES), F32),
        ],
        scratch_shapes=[flat] * 3,
        compiler_params=LIMIT,
        name="signal_grad",
    )(cotan, filt, *tables)


def filter_grad(signal, cotan_spec, grad_signal, blocks, tables):
    rows = signal.shape[0]
    flat = pltpu.VMEM((rows, LANES), F32)
    return pl.pallas_call(
        functools.partial(filter_grad_kernel, blocks, rows // blocks),
        in_specs=[VMEM] * (3 + len(tables)),
        out_specs=[VMEM] * 2,
        out_shape=[
            jax.ShapeDtypeStruct((rows, LANES), BF16),
            jax.ShapeDtypeStruct((rows // blocks, LANES), F32),
        ],
        scratch_shapes=[flat] * 2,
        compiler_params=LIMIT,
        name="filter_grad",
    )(signal, cotan_spec, grad_signal, *tables)


def swapped(rows):
    return lax.all_to_all(rows, "ctx", split_axis=0, concat_axis=0, tiled=True)


def shifted(block, distance):
    devices = range(lax.axis_size("ctx"))
    route = [(i - distance, i) for i in devices if i - distance in devices]
    return lax.ppermute(block, "ctx", route)


def local(query_mr, key_mr, value_mr, key_li, cotangent, norm_gain, filter_mr, filter_li):
    blocks = lax.axis_size("ctx")
    rows = query_mr.shape[0]
    short = short_tables()
    long = long_tables(blocks)
    product = (key_mr.astype(F32) * value_mr.astype(F32)).astype(BF16)
    prior = shifted(product, 1)
    moved_cotan = swapped(cotangent)
    moved_filter = swapped(filter_li.astype(BF16))
    conv, mixed, scaled, gated, window_spec, taps_spec, squares = mr_forward(
        key_mr, value_mr, prior, query_mr, key_li, norm_gain[:, None], filter_mr, short
    )
    inv_rms = lax.rsqrt(lax.psum(squares, "ch") / D + EPSILON)
    signal = (scaled * inv_rms * key_li.astype(F32)).astype(BF16)
    moved_signal = swapped(signal)
    grad_moved, cotan_spec = signal_grad(moved_cotan, moved_filter, blocks, long)
    grad_signal = swapped(grad_moved)
    filter_grad_moved, gain_terms = filter_grad(
        moved_signal, cotan_spec, grad_moved, blocks, long
    )
    grad_filter_li = swapped(filter_grad_moved).astype(F32)

    grad_f = grad_signal.astype(F32)
    grad_key_li = (grad_f * (scaled * inv_rms)).astype(BF16)
    project = lax.psum(
        jnp.sum(grad_f * gated * (mixed.astype(F32) * inv_rms), axis=0, keepdims=True), "ch"
    )
    grad_query, taps_grad, before_grad, own_grad = mr_backward(
        grad_signal, gated, mixed, conv, query_mr, inv_rms, project / D, window_spec, taps_spec,
        short,
    )
    after = shifted(before_grad, -1)
    grad_product = own_grad + after.astype(F32)
    grad_key = (grad_product * value_mr.astype(F32)).astype(BF16)
    grad_value = (grad_product * key_mr.astype(F32)).astype(BF16)

    taps_sum = jnp.sum(swapped(taps_grad).reshape(blocks, -1, LANES).astype(F32), axis=0)
    gain_sum = jnp.sum(gain_terms, axis=1).reshape(1, -1)
    gain_row = jnp.pad(gain_sum, ((0, 7), (0, LANES - gain_sum.shape[1])))
    gathered = lax.all_gather(
        jnp.concatenate([taps_sum, gain_row], axis=0), "ctx", axis=0, tiled=False
    )
    width = rows // blocks
    grad_filter_mr = gathered[:, :width].reshape(rows, LANES)
    grad_gain = gathered[:, width, :width].reshape(rows) / norm_gain
    return (
        grad_query,
        grad_key,
        grad_value,
        grad_key_li,
        grad_gain,
        grad_filter_mr,
        grad_filter_li,
    )


def solution(mesh):
    in_specs = (
        P("ch", "ctx"),
        P("ch", "ctx"),
        P("ch", "ctx"),
        P("ch", "ctx"),
        P("ch", "ctx"),
        P("ch"),
        P("ch", None),
        P("ch", "ctx"),
    )
    out_specs = (
        P("ch", "ctx"),
        P("ch", "ctx"),
        P("ch", "ctx"),
        P("ch", "ctx"),
        P("ch"),
        P("ch", None),
        P("ch", "ctx"),
    )
    return jax.shard_map(local, mesh=mesh, in_specs=in_specs, out_specs=out_specs, check_vma=False)
```

time: 1550 us -> 266 us (0.17)
  the two profiles are of different devices: /device:TPU:8 before, /device:TPU:1 now
where the time goes in v1:
time: 266 us; the launch traced here: 264 us
  waiting for transfers between devices  94.6 us (36%)
  starting transfers between devices  57.1 us (21%)
  Pallas kernels  40.9 us (15%)
  blocking collectives  38.9 us (15%)
  between operations  14.2 us (5%)
  other arithmetic  13.9 us (5%)
  local copies, waits for them, and re-layouts  4.79 us (2%)
    all_to_all x5, starting transfers between devices, swapped(): return lax.all_to_all(rows, 'ctx', split_axis=0, concat_axis=0, tiled=True)  51.3 us
    all_gather x1, waiting for transfers between devices, local(): lax.all_gather(jnp.concatenate([taps_sum, gain_row], axis=0), 'ctx', axis...  45.3 us
    all_to_all x5, waiting for transfers between devices, swapped(): return lax.all_to_all(rows, 'ctx', split_axis=0, concat_axis=0, tiled=True)  38.3 us
    all_to_all x1, blocking collectives, swapped(): return lax.all_to_all(rows, 'ctx', split_axis=0, concat_axis=0, tiled=True)  23.4 us
    pallas_call x1, Pallas kernels, signal_grad(): pl.pallas_call(functools.partial(signal_grad_kernel, blocks, rows // bloc...  11.2 us
    ppermute x2, waiting for transfers between devices, shifted(): return lax.ppermute(block, 'ctx', route)  11 us
    pallas_call x1, Pallas kernels, filter_grad(): pl.pallas_call(functools.partial(filter_grad_kernel, blocks, rows // bloc...  10.2 us
    pallas_call x1, Pallas kernels, mr_forward(): pl.pallas_call(mr_forward_kernel, grid=(rows // ROWS,), in_specs=[row_spe...  10.2 us
  transfers between devices with their start and end apart: 8, of which 7 were waited for; matrix products, arithmetic and copies ran while one was open for 4% of the time, Pallas kernels for 11%

profile of v1, /device:TPU:1, one launch (start us, length us, event | category | flops | bytes accessed | tf_op | source)
XLA Modules:
  0.0 264.4 jit_solution(16317983335941777644)
XLA Ops:
  7.3 13.1 %all-to-all-start = ((bf16[64,32,128]{2,1,0:T(8,128)(2,1)}), bf16[64,32,128]{2,1,0:T(8,128)(2,1)S(1)}, u32[]{:S(2)}, u32[]{:S(2)}) async-start(bf16[64,32,128]{2,1,0:T(8,128)(2,1)} %bitcast.31), calls=%async_computation | async-start | bytes 1048576 | tf_op jit(solution)/shard_map/all_to_all | solution.py:312
  20.4 1.3 convert_element_type.49
  21.7 16.0 %all-to-all-done = bf16[64,32,128]{2,1,0:T(8,128)(2,1)S(1)} async-done(((bf16[64,32,128]{2,1,0:T(8,128)(2,1)}), bf16[64,32,128]{2,1,0:T(8,128)(2,1)S(1)}, u32[]{:S(2)}, u32[]{:S(2)}) %all-to-all-start) | async-done | bytes 524320 | tf_op jit(solution)/shard_map/all_to_all | solution.py:312
  37.7 23.4 %all_to_all.62 = bf16[64,32,128]{2,1,0:T(8,128)(2,1)S(1)} all-to-all(bf16[64,32,128]{2,1,0:T(8,128)(2,1)S(1)} %bitcast.27), channel_id=1, replica_groups=mesh['ctx'=64,'ch'=4] {'ctx'}, dimensions={0} | all-to-all | bytes 1048576 | tf_op jit(solution)/shard_map/all_to_all | solution.py:312
  61.2 11.2 %signal_grad.1 = (bf16[2048,128]{1,0:T(8,128)(2,1)}, f32[2048,256]{1,0:T(8,128)S(1)}) custom-call(bf16[2048,128]{1,0:T(8,128)(2,1)S(1)} %bitcast.22, bf16[2048,128]{1,0:T(8,128)(2,1)S(1)} %bitcast.23, bf16[128,128]{1,0:T(8,128)(2,1)S(1)} %copy-done.5, f32[64,128]{1,0:T(8,128)S(1)} %copy-done.7, f32[64,128]{1,0:T(8,128)S(1)} %copy-done.6, ...), custom_call_target="tpu_custom_call" | custom-call | tf_op jit(solution)/shard_map/signal_grad/pallas_call | solution.py:280
  72.4 6.3 %all-to-all-start.2 = ((bf16[64,32,128]{2,1,0:T(8,128)(2,1)}), bf16[64,32,128]{2,1,0:T(8,128)(2,1)S(1)}, u32[]{:S(2)}, u32[]{:S(2)}) async-start(bf16[64,32,128]{2,1,0:T(8,128)(2,1)} %bitcast.4), calls=%async_computation.2 | async-start | bytes 1048576 | tf_op jit(solution)/shard_map/all_to_all | solution.py:312
  78.7 2.1 fusion.1
  80.8 3.5 %collective-permute-start = (bf16[2048,128]{1,0:T(8,128)(2,1)}, bf16[2048,128]{1,0:T(8,128)(2,1)}, u32[]{:S(2)}, u32[]{:S(2)}) collective-permute-start(bf16[2048,128]{1,0:T(8,128)(2,1)} %fusion.1), channel_id=1, source_target_pairs={{0,4},{4,8},{8,12},{12,16},{16,20},{20,24},{24,28},{28,32},{32,36}... | collective-permute-start | bytes 1572872 | tf_op jit(solution)/shard_map/ppermute | solution.py:318
  84.3 1.3 copy.31.gain
  85.7 10.3 %collective-permute-done.prior = bf16[2048,128]{1,0:T(8,128)(2,1)} collective-permute-done((bf16[2048,128]{1,0:T(8,128)(2,1)}, bf16[2048,128]{1,0:T(8,128)(2,1)}, u32[]{:S(2)}, u32[]{:S(2)}) %collective-permute-start) | collective-permute-done | bytes 524320 | tf_op jit(solution)/shard_map/ppermute | solution.py:318
  96.0 10.2 %mr_forward.1 = (f32[2048,128]{1,0:T(8,128)}, bf16[2048,128]{1,0:T(8,128)(2,1)}, f32[2048,128]{1,0:T(8,128)}, f32[2048,128]{1,0:T(8,128)}, f32[2048,256]{1,0:T(8...) custom-call(bf16[2048,128]{1,0:T(8,128)(2,1)} %key.1, bf16[2048,128]{1,0:T(8,128)(2,1)} %value.1, ...), custom_call_target="tpu_custom_call" | custom-call | tf_op jit(solution)/shard_map/mr_forward/pallas_call | solution.py:143
  106.2 8.9 %psum.14 = f32[1,128]{1,0:T(1,128)S(1)} all-reduce(f32[1,128]{1,0:T(1,128)} %get-tuple-element.26), channel_id=1, replica_groups=mesh['ctx'=64,'ch'=4] {'ch'}, use_global_device_ids=true, to_apply=%region_0.0 | all-reduce | flops 128 | bytes 1024 | tf_op jit(solution)/shard_map/psum | solution.py:333
  115.6 3.4 %multiply_convert_fusion = (bf16[2048,128]{1,0:T(8,128)(2,1)}, bf16[2048,128]{1,0:T(8,128)(2,1)}, f32[128]{0:T(128)S(1)}) fusion(bf16[2048,128]{1,0:T(8,128)(2,1)} %key_li.1, f32[2048,128]{1,0:T(8,128)} %get-tuple-element.32, f32[128]{0:T(128)S(1)} %get-tuple-element.42, bf16[64,32,128]{2,1,0:T(8,128)(2,1)S(1)} %all-to-all-done.2, ...), kind=kLoop, calls=%fused_computation.11 | loop fusion | flops 3145600 | bytes 4719616 | tf_op jit(solution)/shard_map/convert_element_type | solution.py:334
  119.0 13.4 %all-to-all-start.4 = ((bf16[64,32,128]{2,1,0:T(8,128)(2,1)}), bf16[64,32,128]{2,1,0:T(8,128)(2,1)S(1)}, u32[]{:S(2)}, u32[]{:S(2)}) async-start(bf16[64,32,128]{2,1,0:T(8,128)(2,1)} %bitcast.26), calls=%async_computation.4 | async-start | bytes 1048576 | tf_op jit(solution)/shard_map/all_to_all | solution.py:312
  132.4 6.6 %psum.15 = f32[1,128]{1,0:T(1,128)S(1)} all-reduce(f32[1,128]{1,0:T(1,128)S(1)} %bitcast.35), channel_id=1, replica_groups=mesh['ctx'=64,'ch'=4] {'ch'}, use_global_device_ids=true, to_apply=%region_2.0 | all-reduce | flops 128 | bytes 1024 | tf_op jit(solution)/shard_map/psum | solution.py:345
  139.6 9.3 %mr_backward.1 = (bf16[2048,128]{1,0:T(8,128)(2,1)}, bf16[2048,128]{1,0:T(8,128)(2,1)}, bf16[2048,128]{1,0:T(8,128)(2,1)}, f32[2048,128]{1,0:T(8,128)}) custom-call(bf16[2048,128]{1,0:T(8,128)(2,1)} %bitcast.25, f32[2048,128]{1,0:T(8,128)} %get-tuple-element.23.gated, bf16[2048,128]{1,0:T(8,128)(2,1)} %get-tuple-element.24.mixed, ...), custom_call_target="tpu_custom_call" | custom-call | tf_op jit(solution)/shard_map/mr_backward/pallas_call | solution.py:160
  148.8 0.9 all-to-all-done.4
  149.7 10.8 %all-to-all-start.3 = ((bf16[64,32,128]{2,1,0:T(8,128)(2,1)}), bf16[64,32,128]{2,1,0:T(8,128)(2,1)}, u32[]{:S(2)}, u32[]{:S(2)}) async-start(bf16[64,32,128]{2,1,0:T(8,128)(2,1)} %bitcast.32), calls=%async_computation.3 | async-start | bytes 1048576 | tf_op jit(solution)/shard_map/all_to_all | solution.py:312
  160.6 10.2 %filter_grad.1 = (bf16[2048,128]{1,0:T(8,128)(2,1)}, f32[32,128]{1,0:T(8,128)S(1)}) custom-call(bf16[2048,128]{1,0:T(8,128)(2,1)S(1)} %bitcast.24, f32[2048,256]{1,0:T(8,128)S(1)} %get-tuple-element.34.cotan_spec, bf16[2048,128]{1,0:T(8,128)(2,1)} %get-tuple-element.22.grad_signal, bf16[128,128]{1,0:T(8,128)(2,1)S(1)} %copy-done.5, f32[64,128]{1,0:T(8,128)S(1)} %copy-done.7, ...), custom_call_target="tpu_custom_call" | custom-call | tf_op jit(solution)/shard_map/filter_grad/pallas_call | solution.py:297
  170.9 6.8 %all-to-all-done.3 = bf16[64,32,128]{2,1,0:T(8,128)(2,1)} async-done(((bf16[64,32,128]{2,1,0:T(8,128)(2,1)}), bf16[64,32,128]{2,1,0:T(8,128)(2,1)}, u32[]{:S(2)}, u32[]{:S(2)}) %all-to-all-start.3) | async-done | bytes 524320 | tf_op jit(solution)/shard_map/all_to_all | solution.py:312
  177.8 1.1 convert_reduce_fusion
  178.9 0.6 select_maximum_fusion
  179.5 2.2 collective-permute-start.1
  181.8 7.8 %all-to-all-start.5 = ((bf16[64,32,128]{2,1,0:T(8,128)(2,1)}), bf16[64,32,128]{2,1,0:T(8,128)(2,1)S(1)}, u32[]{:S(2)}, u32[]{:S(2)}) async-start(bf16[64,32,128]{2,1,0:T(8,128)(2,1)} %bitcast.15), calls=%async_computation.5 | async-start | bytes 1048576 | tf_op jit(solution)/shard_map/all_to_all | solution.py:312
  189.5 0.7 collective-permute-done.1
  190.3 2.4 fusion
  192.7 14.5 %all-to-all-done.5 = bf16[64,32,128]{2,1,0:T(8,128)(2,1)S(1)} async-done(((bf16[64,32,128]{2,1,0:T(8,128)(2,1)}), bf16[64,32,128]{2,1,0:T(8,128)(2,1)S(1)}, u32[]{:S(2)}, u32[]{:S(2)}) %all-to-all-start.5) | async-done | bytes 524320 | tf_op jit(solution)/shard_map/all_to_all | solution.py:312
  207.2 1.1 bitcast_convert_fusion
  208.3 45.3 %all-gather.3.cloned.1.call-done = f32[2560,128]{1,0:T(8,128)} async-done(((f32[40,128]{1,0:T(8,128)}), f32[2560,128]{1,0:T(8,128)}) %all-gather.3.cloned.1.call-update) | async-done | bytes 1310736 | tf_op jit(solution)/shard_map/all_gather | solution.py:360
  253.6 1.0 slice_reduce_fusion
  254.6 2.3 slice.9
  257.0 0.6 div.11
  (29 shorter events, 1.4 us)
Async XLA Ops:
  7.2 54.0 %copy-start.4 = (bf16[64,384]{1,0:T(8,128)(2,1)S(1)}, bf16[64,384]{1,0:T(8,128)(2,1)}, u32[]{:S(2)}) copy-start(bf16[64,384]{1,0:T(8,128)(2,1)} %constant.55.last) | copy-start | bytes 147460
  7.2 53.9 %copy-start.5 = (bf16[128,128]{1,0:T(8,128)(2,1)S(1)}, bf16[128,128]{1,0:T(8,128)(2,1)}, u32[]{:S(2)}) copy-start(bf16[128,128]{1,0:T(8,128)(2,1)} %constant.54.first) | copy-start | bytes 98308
  7.2 53.9 %copy-start = (bf16[256,256]{1,0:T(8,128)(2,1)S(1)}, bf16[256,256]{1,0:T(8,128)(2,1)}, u32[]{:S(2)}) copy-start(bf16[256,256]{1,0:T(8,128)(2,1)} %constant.51.clone.back_low) | copy-start | bytes 393220
  7.2 53.9 %copy-start.1 = (bf16[256,256]{1,0:T(8,128)(2,1)S(1)}, bf16[256,256]{1,0:T(8,128)(2,1)}, u32[]{:S(2)}) copy-start(bf16[256,256]{1,0:T(8,128)(2,1)} %constant.50.clone.back_high) | copy-start | bytes 393220
  7.2 53.9 %copy-start.2 = (bf16[256,256]{1,0:T(8,128)(2,1)S(1)}, bf16[256,256]{1,0:T(8,128)(2,1)}, u32[]{:S(2)}) copy-start(bf16[256,256]{1,0:T(8,128)(2,1)} %constant.49.clone.low) | copy-start | bytes 393220
  7.2 53.9 %copy-start.3 = (bf16[256,256]{1,0:T(8,128)(2,1)S(1)}, bf16[256,256]{1,0:T(8,128)(2,1)}, u32[]{:S(2)}) copy-start(bf16[256,256]{1,0:T(8,128)(2,1)} %constant.48.clone.high) | copy-start | bytes 393220
  7.2 53.9 %copy-start.6 = (f32[64,128]{1,0:T(8,128)S(1)}, f32[64,128]{1,0:T(8,128)}, u32[]{:S(2)}) copy-start(f32[64,128]{1,0:T(8,128)} %constant.47.clone.sine) | copy-start | bytes 98308
  7.3 53.9 %copy-start.7 = (f32[64,128]{1,0:T(8,128)S(1)}, f32[64,128]{1,0:T(8,128)}, u32[]{:S(2)}) copy-start(f32[64,128]{1,0:T(8,128)} %constant.46.clone.cosine) | copy-start | bytes 98308
  7.3 30.5 %all-to-all-start = ((bf16[64,32,128]{2,1,0:T(8,128)(2,1)}), bf16[64,32,128]{2,1,0:T(8,128)(2,1)S(1)}, u32[]{:S(2)}, u32[]{:S(2)}) async-start(bf16[64,32,128]{2,1,0:T(8,128)(2,1)} %bitcast.31), calls=%async_computation | async-start | bytes 1048576 | tf_op jit(solution)/shard_map/all_to_all | solution.py:312
  61.2 23.2 %copy-start.10 = (f32[2048]{0:T(1024)S(1)}, f32[2048]{0:T(1024)}, u32[]{:S(2)}) copy-start(f32[2048]{0:T(1024)} %param.27) | copy-start | bytes 24580
  72.4 43.2 %all-to-all-start.2 = ((bf16[64,32,128]{2,1,0:T(8,128)(2,1)}), bf16[64,32,128]{2,1,0:T(8,128)(2,1)S(1)}, u32[]{:S(2)}, u32[]{:S(2)}) async-start(bf16[64,32,128]{2,1,0:T(8,128)(2,1)} %bitcast.4), calls=%async_computation.2 | async-start | bytes 1048576 | tf_op jit(solution)/shard_map/all_to_all | solution.py:312
  80.8 15.2 %collective-permute-start = (bf16[2048,128]{1,0:T(8,128)(2,1)}, bf16[2048,128]{1,0:T(8,128)(2,1)}, u32[]{:S(2)}, u32[]{:S(2)}) collective-permute-start(bf16[2048,128]{1,0:T(8,128)(2,1)} %fusion.1), channel_id=1, source_target_pairs={{0,4},{4,8},{8,12},{12,16},{16,20},{20,24},{24,28},{28,32},{32,36}... | collective-permute-start | bytes 1572872 | tf_op jit(solution)/shard_map/ppermute | solution.py:318
  115.6 3.4 %copy-start.8 = (bf16[64,32,128]{2,1,0:T(8,128)(2,1)}, bf16[64,32,128]{2,1,0:T(8,128)(2,1)S(1)}, u32[]{:S(2)}) copy-start(bf16[64,32,128]{2,1,0:T(8,128)(2,1)S(1)} %all-to-all-done.2) | copy-start | bytes 1572868
  119.0 30.7 %all-to-all-start.4 = ((bf16[64,32,128]{2,1,0:T(8,128)(2,1)}), bf16[64,32,128]{2,1,0:T(8,128)(2,1)S(1)}, u32[]{:S(2)}, u32[]{:S(2)}) async-start(bf16[64,32,128]{2,1,0:T(8,128)(2,1)} %bitcast.26), calls=%async_computation.4 | async-start | bytes 1048576 | tf_op jit(solution)/shard_map/all_to_all | solution.py:312
  149.7 28.0 %all-to-all-start.3 = ((bf16[64,32,128]{2,1,0:T(8,128)(2,1)}), bf16[64,32,128]{2,1,0:T(8,128)(2,1)}, u32[]{:S(2)}, u32[]{:S(2)}) async-start(bf16[64,32,128]{2,1,0:T(8,128)(2,1)} %bitcast.32), calls=%async_computation.3 | async-start | bytes 1048576 | tf_op jit(solution)/shard_map/all_to_all | solution.py:312
  160.5 93.1 %all-gather.3.cloned.1.call-start = ((), (), s32[]{:S(2)}) async-start(), calls=%async_computation.6 | async-start | bytes 1331200 | tf_op jit(solution)/shard_map/all_gather | solution.py:360
  170.8 19.4 %copy-start.9 = (f32[2048,128]{1,0:T(8,128)S(1)}, f32[2048,128]{1,0:T(8,128)}, u32[]{:S(2)}) copy-start(f32[2048,128]{1,0:T(8,128)} %get-tuple-element.30) | copy-start | bytes 3145732
  179.5 10.7 %collective-permute-start.1 = (bf16[2048,128]{1,0:T(8,128)(2,1)}, bf16[2048,128]{1,0:T(8,128)(2,1)S(1)}, u32[]{:S(2)}, u32[]{:S(2)}) collective-permute-start(bf16[2048,128]{1,0:T(8,128)(2,1)} %get-tuple-element.31), channel_id=1, source_target_pairs={{4,0},{8,4},{12,8},{16,12},{20,16},{24,20},{28,24},{32,28},{36,32}... | collective-permute-start | bytes 1572872 | tf_op jit(solution)/shard_map/ppermute | solution.py:318
  181.8 25.4 %all-to-all-start.5 = ((bf16[64,32,128]{2,1,0:T(8,128)(2,1)}), bf16[64,32,128]{2,1,0:T(8,128)(2,1)S(1)}, u32[]{:S(2)}, u32[]{:S(2)}) async-start(bf16[64,32,128]{2,1,0:T(8,128)(2,1)} %bitcast.15), calls=%async_computation.5 | async-start | bytes 1048576 | tf_op jit(solution)/shard_map/all_to_all | solution.py:312
Sparse Core Ops, SparseCore 0:
  179.7 73.8 all-gather.2
